TPU v7x, 256 devices: a whole 4x4x8 slice. The times are simulated.
256 devices in a mesh: prow: 32 (over x, z), pcol: 8 (over y, core).
Axes of the slice: x: 4, y: 4, z: 8, core: 2. Of those that a mesh axis runs over, the one named last changes fastest.
Arguments:
- matrix: float32 [24, 512, 3, 4096], P(None, 'prow', None, 'pcol'), may hold values from -6 to 6
- pivots: int32 [2, 512], replicated, may hold values from 0 to 12287, as said below
- lower_inv: float32 [2, 512, 512], replicated
- upper_inv: float32 [2, 512, 512], replicated
Outputs:
- factored: float32 [24, 512, 3, 4096], P(None, 'prow', None, 'pcol')
Inputs may be any that keep to these rules, and one draw needn't show every extreme that they name: pivots[k, i] is at least k * 512 + i; every panel has one entry equal to 12287, and the first panel's first row keeps its place.
All inputs are finite; a program needn't handle non-finite values.
Results may differ from a plain program's by a relative error of at most 0.00011.
Values sent between devices are 32-bit elements; how exact they have to be, the bound alone decides.
A program may use at most 64 MiB of HBM per device.

v0:
```python
import jax
import jax.numpy as jnp
from jax import lax
from jax.sharding import Mesh
from jax.sharding import PartitionSpec as P

PROW = ("prow_0", "prow_1")


def in_order(parts, dim):
    shape = list(parts.shape[1:])
    shape[dim] *= parts.shape[0]
    return jnp.moveaxis(parts, 0, dim).reshape(shape)


def all_blocks(x, axes, order):
    parts = x
    for k in order:
        parts = lax.all_gather(parts, axes[k])
    done = order[::-1]
    back = [done.index(k) for k in range(len(axes))]
    parts = parts.transpose(*back, *range(len(axes), parts.ndim))
    return parts.reshape(-1, *x.shape)


def gathered_by_axis(x, axes, order, dim):
    return in_order(all_blocks(x, axes, order), dim)


def sum_by_axis(x, axes, dim):
    for axis in axes:
        x = lax.psum_scatter(x, axis, scatter_dimension=dim, tiled=True)
    return x


def broadcast(x, axis, root):
    return lax.dynamic_index_in_dim(lax.all_gather(x, axis), root, 0, keepdims=False)


def permutation(pivot_row, offset, panel_width, full_order):
    steps = jnp.arange(panel_width, dtype=jnp.int32)
    anchors = offset + steps
    earlier = steps[None, :] < steps[:, None]
    hits_anchor = (pivot_row[None, :] == anchors[:, None]) & earlier
    chain_from = jnp.max(jnp.where(hits_anchor, steps[None, :], -1), axis=1)
    pointer = jnp.where(chain_from >= 0, chain_from, steps)
    for level in range(max(1, panel_width.bit_length())):
        pointer = pointer[pointer]
    before_value = offset + pointer
    same_target = (pivot_row[None, :] == pivot_row[:, None]) & earlier
    last_before = jnp.max(jnp.where(same_target, steps[None, :], -1), axis=1)
    anchor_value = jnp.where(
        last_before >= 0, before_value[jnp.clip(last_before, 0, panel_width - 1)], pivot_row
    )
    later = steps[None, :] > steps[:, None]
    has_later = jnp.any((pivot_row[None, :] == pivot_row[:, None]) & later, axis=1)
    outside = jnp.logical_not(has_later) & (pivot_row >= offset + panel_width)
    spots = jnp.where(outside, pivot_row, full_order)
    ordering = jnp.arange(full_order, dtype=jnp.int32).at[spots].set(before_value, mode="drop")
    return lax.dynamic_update_slice_in_dim(ordering, anchor_value, offset, 0)


def product(left, right):
    return jnp.dot(left, right, precision=lax.Precision.HIGHEST, preferred_element_type=jnp.float32)


def local(matrix, pivots, lower_inv, upper_inv):
    row_blocks, row_part, col_blocks, col_part = matrix.shape
    panel_width = lower_inv.shape[1]
    panel_count = pivots.shape[0]
    full_order = row_blocks * panel_width
    row_devices = lax.axis_size(PROW)
    col_devices = lax.axis_size("pcol")
    row_index = lax.axis_index(PROW)
    col_index = lax.axis_index("pcol")
    local_rows = row_blocks * row_part
    local_cols = col_blocks * col_part
    share_width = local_cols // row_devices
    current = matrix.reshape(local_rows, local_cols)
    global_rows = (
        jnp.arange(row_blocks, dtype=jnp.int32)[:, None] * panel_width
        + row_index * row_part
        + jnp.arange(row_part, dtype=jnp.int32)[None, :]
    ).reshape(local_rows)
    col_span = col_devices * col_part
    global_cols = (
        jnp.arange(col_blocks, dtype=jnp.int32)[:, None] * col_span
        + col_index * col_part
        + jnp.arange(col_part, dtype=jnp.int32)[None, :]
    ).reshape(local_cols)
    for panel_index in range(panel_count):
        offset = panel_index * panel_width
        ending = offset + panel_width
        ordering = permutation(pivots[panel_index], offset, panel_width, full_order)
        source = ordering[global_rows]
        old_top = current[panel_index * row_part : (panel_index + 1) * row_part]
        old_panel = gathered_by_axis(old_top, PROW, (0, 1), 0)
        wanted = ordering[offset + jnp.arange(panel_width, dtype=jnp.int32)]
        holder = wanted % panel_width // row_part
        local_spot = wanted // panel_width * row_part + wanted % row_part
        picked = jnp.where((holder == row_index)[:, None], current[local_spot], 0.0)
        column_share = sum_by_axis(picked, PROW, 1)
        share_cols = lax.dynamic_slice_in_dim(global_cols, row_index * share_width, share_width)
        solved = product(lower_inv[panel_index], column_share)
        merged = jnp.where((share_cols >= ending)[None, :], solved, column_share)
        top_rows = gathered_by_axis(merged, PROW, (0, 1), 1)
        in_panel = global_rows // panel_width == panel_index
        displaced = (source != global_rows) & jnp.logical_not(in_panel)
        from_old = old_panel[jnp.clip(source - offset, 0, panel_width - 1)]
        current = jnp.where(displaced[:, None], from_old, current)
        own_rows = lax.dynamic_slice_in_dim(top_rows, row_index * row_part, row_part, 0)
        current = lax.dynamic_update_slice_in_dim(current, own_rows, panel_index * row_part, 0)
        trailing_row = global_rows >= ending
        trailing_col = global_cols >= ending
        lower_full = product(current[:, :col_part], upper_inv[panel_index])
        lower_here = jnp.where(trailing_row[:, None], lower_full, 0.0)
        lower_rows = broadcast(lower_here, "pcol", panel_index)
        upper_part = jnp.where(trailing_col[None, :], top_rows, 0.0)
        current = current - product(lower_rows, upper_part)
        own_panel = col_index == panel_index
        new_cols = jnp.where(own_panel & trailing_row[:, None], lower_rows, current[:, :col_part])
        current = jnp.concatenate([new_cols, current[:, col_part:]], axis=1)
    return current.reshape(row_blocks, row_part, col_blocks, col_part)


def solution(mesh):
    finer = Mesh(mesh.devices.reshape(4, 8, mesh.shape["pcol"]), ("prow_0", "prow_1", "pcol"))
    in_specs = (P(None, PROW, None, "pcol"), P(), P(), P())
    out_specs = P(None, PROW, None, "pcol")
    return jax.shard_map(local, mesh=finer, in_specs=in_specs, out_specs=out_specs, check_vma=False)
```

profile of v0, /device:TPU:8, one launch (start us, length us, event | category | flops | bytes accessed | tf_op | source)
XLA Modules:
  0.0 634.8 jit_solution(12311615497677265065)
XLA Ops:
  8.4 3.5 gather_fusion.12
  11.9 3.5 gather_fusion.13
  15.5 3.5 gather_fusion.14
  19.0 3.5 gather_fusion.15
  22.5 3.5 gather_fusion.16
  26.1 3.5 gather_fusion.17
  29.6 3.5 gather_fusion.18
  33.1 3.5 gather_fusion.19
  36.6 3.5 gather_fusion.20
  40.2 3.5 gather_fusion.21
  47.2 3.5 gather_fusion
  50.7 3.5 gather_fusion.1
  54.2 3.5 gather_fusion.2
  57.7 3.5 gather_fusion.3
  61.3 3.5 gather_fusion.4
  64.8 3.5 gather_fusion.5
  68.3 3.5 gather_fusion.6
  71.8 3.5 gather_fusion.7
  75.4 3.5 gather_fusion.8
  78.9 3.5 gather_fusion.9
  82.5 3.5 gather_fusion.22
  89.0 3.5 gather_fusion.10
  95.0 3.1 gather_fusion.28
  104.4 3.6 copy.39
  108.0 4.0 broadcast_select_fusion.1
  112.0 43.8 %reduce-scatter.5.cloned.1.call-done = f32[512,384]{0,1:T(8,128)} async-done(((f32[512,1536]{0,1:T(8,128)}), f32[512,384]{0,1:T(8,128)}) %reduce-scatter.5.cloned.1.call-update) | async-done | bytes 786448 | tf_op jit(solution)/shard_map/reduce_scatter | solution.py:32
  156.8 13.8 %all_gather.61 = f32[4,16,1536]{2,1,0:T(8,128)} all-gather(f32[1,16,1536]{2,1,0:T(8,128)S(1)} %bitcast.164), channel_id=1, replica_groups=mesh['prow_0'=4,'prow_1'=8,'pcol'=8] {'prow_0'}, dimensions={0}, use_global_device_ids=true | all-gather | bytes 491520 | tf_op jit(solution)/shard_map/all_gather | solution.py:19
  170.8 25.2 %reduce-scatter.7.cloned.1.call-done = f32[512,48]{0,1:T(8,128)} async-done(((f32[512,384]{0,1:T(8,128)}), f32[512,48]{0,1:T(8,128)}) %reduce-scatter.7.cloned.1.call-update) | async-done | bytes 98320 | tf_op jit(solution)/shard_map/reduce_scatter | solution.py:32
  198.3 12.8 %all-gather.1 = f32[2048,48]{0,1:T(8,128)S(1)} all-gather(f32[512,48]{0,1:T(8,128)S(1)} %fusion.1), channel_id=3, replica_groups=mesh['prow_0'=4,'prow_1'=8,'pcol'=8] {'prow_0'}, dimensions={0}, use_global_device_ids=true | all-gather | bytes 491520 | tf_op jit(solution)/shard_map/all_gather | solution.py:19
  217.4 24.1 %all-gather.16.cloned.1.call-done = f32[32,16,1536]{2,1,0:T(8,128)} async-done(((f32[4,16,1536]{2,1,0:T(8,128)}), f32[32,16,1536]{2,1,0:T(8,128)}) %all-gather.16.cloned.1.call-update) | async-done | bytes 3145744 | tf_op jit(solution)/shard_map/all_gather | solution.py:19
  241.5 3.9 copy.37
  245.4 6.2 gather_fusion.24
  251.6 3.4 broadcast_select_fusion.2
  254.9 32.0 %all-gather.18.cloned.1.call-done = f32[32,512,48]{1,2,0:T(8,128)} async-done(((f32[4,512,48]{1,2,0:T(8,128)}), f32[32,512,48]{1,2,0:T(8,128)}) %all-gather.18.cloned.1.call-update) | async-done | bytes 3145744 | tf_op jit(solution)/shard_map/all_gather | solution.py:19
  292.4 3.8 convolution_select_fusion.1
  298.6 38.9 %all-gather.20.cloned.1.call-done = f32[3072,512]{1,0:T(8,128)} async-done(((f32[384,512]{1,0:T(8,128)}), f32[3072,512]{1,0:T(8,128)}) %all-gather.20.cloned.1.call-update) | async-done | bytes 6291472 | tf_op jit(solution)/shard_map/all_gather | solution.py:37
  337.6 7.0 %convolution_subtract_fusion.1 = f32[384,1536]{1,0:T(8,128)S(1)} fusion(f32[384,1536]{1,0:T(8,128)} %constant_dynamic-update-slice_fusion.1, f32[512,1536]{0,1:T(8,128)} %bitcast.152, f32[3072,512]{1,0:T(8,128)} %all-gather.20.cloned.1.call-done), kind=kOutput, calls=%fused_computation.35 | convolution fusion | flops 3624468480 | bytes 8650752 | tf_op jit(solution)/shard_map/dot_general | solution.py:64
  346.6 13.6 %all-gather.4 = f32[64,1536]{1,0:T(8,128)} all-gather(f32[16,1536]{1,0:T(8,128)S(1)} %fusion.18), channel_id=6, replica_groups=mesh['prow_0'=4,'prow_1'=8,'pcol'=8] {'prow_0'}, dimensions={0}, use_global_device_ids=true | all-gather | bytes 491520 | tf_op jit(solution)/shard_map/all_gather | solution.py:19
  360.4 45.7 %all-gather.22.cloned.1.call-done = f32[32,16,1536]{2,1,0:T(8,128)} async-done(((f32[4,16,1536]{2,1,0:T(8,128)}), f32[32,16,1536]{2,1,0:T(8,128)}) %all-gather.22.cloned.1.call-update) | async-done | bytes 3145744 | tf_op jit(solution)/shard_map/all_gather | solution.py:19
  410.9 4.1 pad_maximum_fusion
  422.5 39.5 %reduce-scatter.9.cloned.1.call-done = f32[512,384]{0,1:T(8,128)} async-done(((f32[512,1536]{0,1:T(8,128)}), f32[512,384]{0,1:T(8,128)}) %reduce-scatter.9.cloned.1.call-update) | async-done | bytes 786448 | tf_op jit(solution)/shard_map/reduce_scatter | solution.py:32
  462.1 40.3 %reduce-scatter.11.cloned.1.call-done = f32[512,48]{0,1:T(8,128)} async-done(((f32[512,384]{0,1:T(8,128)}), f32[512,48]{0,1:T(8,128)}) %reduce-scatter.11.cloned.1.call-update) | async-done | bytes 98320 | tf_op jit(solution)/shard_map/reduce_scatter | solution.py:32
  504.4 12.8 %all-gather.6 = f32[2048,48]{0,1:T(8,128)S(1)} all-gather(f32[512,48]{0,1:T(8,128)S(1)} %fusion), channel_id=8, replica_groups=mesh['prow_0'=4,'prow_1'=8,'pcol'=8] {'prow_0'}, dimensions={0}, use_global_device_ids=true | all-gather | bytes 491520 | tf_op jit(solution)/shard_map/all_gather | solution.py:19
  518.3 42.9 %all-gather.24.cloned.1.call-done = f32[32,512,48]{1,2,0:T(8,128)} async-done(((f32[4,512,48]{1,2,0:T(8,128)}), f32[32,512,48]{1,2,0:T(8,128)}) %all-gather.24.cloned.1.call-update) | async-done | bytes 3145744 | tf_op jit(solution)/shard_map/all_gather | solution.py:19
  566.7 3.8 convolution_select_fusion
  572.6 39.2 %all-gather.26.cloned.1.call-done = f32[3072,512]{1,0:T(8,128)} async-done(((f32[384,512]{1,0:T(8,128)}), f32[3072,512]{1,0:T(8,128)}) %all-gather.26.cloned.1.call-update) | async-done | bytes 6291472 | tf_op jit(solution)/shard_map/all_gather | solution.py:37
  611.9 7.0 %convolution_subtract_fusion = f32[384,1536]{1,0:T(8,128)S(1)} fusion(f32[384,1536]{1,0:T(8,128)} %constant_dynamic-update-slice_fusion, f32[512,1536]{0,1:T(8,128)} %bitcast.153, f32[3072,512]{1,0:T(8,128)} %all-gather.26.cloned.1.call-done), kind=kOutput, calls=%fused_computation.34 | convolution fusion | flops 3624468480 | bytes 8650752 | tf_op jit(solution)/shard_map/dot_general | solution.py:64
  621.9 3.5 reshape.880
  (157 shorter events, 65.3 us)
Async XLA Ops:
  6.5 149.2 %reduce-scatter.5.cloned.1.call-start = ((), (), s32[]{:S(2)}) async-start(), calls=%async_computation.4 | async-start | bytes 3932160 | tf_op jit(solution)/shard_map/reduce_scatter | solution.py:32
  36.6 7.1 %copy-start.2 = (f32[24,16,3,512]{3,1,2,0:T(8,128)S(1)}, f32[24,16,3,512]{3,1,2,0:T(8,128)}, u32[]{:S(2)}) copy-start(f32[24,16,3,512]{3,1,2,0:T(8,128)} %param.4) | copy-start | bytes 7077892
  75.3 7.2 %copy-start.4 = (s32[2,512]{1,0:T(2,128)S(1)}, s32[2,512]{1,0:T(2,128)}, u32[]{:S(2)}) copy-start(s32[2,512]{1,0:T(2,128)} %param.5) | copy-start | bytes 12292
  112.0 84.0 %reduce-scatter.7.cloned.1.call-start = ((), (), s32[]{:S(2)}) async-start(), calls=%async_computation.5 | async-start | bytes 884736 | tf_op jit(solution)/shard_map/reduce_scatter | solution.py:32
  155.8 85.7 %all-gather.16.cloned.1.call-start = ((), (), s32[]{:S(2)}) async-start(), calls=%async_computation.8 | async-start | bytes 3538944 | tf_op jit(solution)/shard_map/all_gather | solution.py:19
  170.5 116.4 %all-gather.18.cloned.1.call-start = ((), (), s32[]{:S(2)}) async-start(), calls=%async_computation.9 | async-start | bytes 3538944 | tf_op jit(solution)/shard_map/all_gather | solution.py:19
  211.9 125.7 %all-gather.20.cloned.1.call-start = ((), (), s32[]{:S(2)}) async-start(), calls=%async_computation.10 | async-start | bytes 7077888 | tf_op jit(solution)/shard_map/all_gather | solution.py:37
  296.2 109.8 %all-gather.22.cloned.1.call-start = ((), (), s32[]{:S(2)}) async-start(), calls=%async_computation.11 | async-start | bytes 3538944 | tf_op jit(solution)/shard_map/all_gather | solution.py:19
  344.7 1.9 copy-start
  346.6 13.6 %copy-start.1 = (f32[384,512]{1,0:T(8,128)}, f32[384,512]{1,0:T(8,128)S(1)}, u32[]{:S(2)}) copy-start(f32[384,512]{1,0:T(8,128)S(1)} %slice_select_fusion.1) | copy-start | bytes 2359300
  360.2 101.8 %reduce-scatter.9.cloned.1.call-start = ((), (), s32[]{:S(2)}) async-start(), calls=%async_computation.6 | async-start | bytes 3932160 | tf_op jit(solution)/shard_map/reduce_scatter | solution.py:32
  422.5 79.9 %copy-start.3 = (f32[2,512,512]{2,1,0:T(8,128)S(1)}, f32[2,512,512]{2,1,0:T(8,128)}, u32[]{:S(2)}) copy-start(f32[2,512,512]{2,1,0:T(8,128)} %param.6) | copy-start | bytes 6291460
  422.5 79.9 %reduce-scatter.11.cloned.1.call-start = ((), (), s32[]{:S(2)}) async-start(), calls=%async_computation.7 | async-start | bytes 884736 | tf_op jit(solution)/shard_map/reduce_scatter | solution.py:32
  462.0 99.2 %all-gather.24.cloned.1.call-start = ((), (), s32[]{:S(2)}) async-start(), calls=%async_computation.12 | async-start | bytes 3538944 | tf_op jit(solution)/shard_map/all_gather | solution.py:19
  518.1 93.8 %all-gather.26.cloned.1.call-start = ((), (), s32[]{:S(2)}) async-start(), calls=%async_computation.13 | async-start | bytes 7077888 | tf_op jit(solution)/shard_map/all_gather | solution.py:37
Sparse Core Ops, SparseCore 0:
  112.1 43.6 reduce-scatter.4
  158.3 37.5 reduce-scatter.6
  197.9 43.5 all-gather.15
  243.3 43.5 all-gather.17
  296.3 41.1 all-gather.19
  360.4 45.6 all-gather.21
  422.6 39.3 reduce-scatter.8
  464.7 37.6 reduce-scatter.10
  518.2 42.9 all-gather.23
  570.6 41.1 all-gather.25
where the time goes:
time: 647 us; the launch traced here: 635 us
  waiting for transfers between devices  372 us (57%)
  local copies, waits for them, and re-layouts  144 us (22%)
  blocking collectives  53 us (8%)
  matrix products  26 us (4%)
  other arithmetic  24.7 us (4%)
  between operations  14.8 us (2%)
    reduce_scatter x4, waiting for transfers between devices, sum_by_axis(): x = lax.psum_scatter(x, axis, scatter_dimension=dim, tiled=True)  149 us
    all_gather x4, waiting for transfers between devices, all_blocks(): parts = lax.all_gather(parts, axes[k])  145 us
    all_gather x2, waiting for transfers between devices, broadcast(): lax.all_gather(x, axis)  78.2 us
    gather x20, local copies, waits for them, and re-layouts, permutation(): pointer = pointer[pointer]  69.8 us
    all_gather x4, blocking collectives, all_blocks(): parts = lax.all_gather(parts, axes[k])  53 us
    dot_general x6, matrix products, product(): jnp.dot(left, right, precision=lax.Precision.HIGHEST, preferred_element_t...  26 us
  transfers between devices with their start and end apart: 10, of which 10 were waited for; matrix products, arithmetic and copies ran while one was open for 4% of the time, Pallas kernels for 0%

commit v1 on v0

--- a/solution.py
+++ b/solution.py
@@ -1,10 +1,17 @@
+import functools
+
 import jax
 import jax.numpy as jnp
 from jax import lax
+from jax.experimental import pallas as pl
+from jax.experimental.pallas import tpu as pltpu
 from jax.sharding import Mesh
 from jax.sharding import PartitionSpec as P
 
-PROW = ("prow_0", "prow_1")
+PROW = ("x", "z")
+MESH = pl.DeviceIdType.MESH
+NX, NZ = 4, 8
+CAP = 56
 
 
 def in_order(parts, dim):
@@ -64,7 +71,7 @@
     return jnp.dot(left, right, precision=lax.Precision.HIGHEST, preferred_element_type=jnp.float32)
 
 
-def local(matrix, pivots, lower_inv, upper_inv):
+def general(matrix, pivots, lower_inv, upper_inv):
     row_blocks, row_part, col_blocks, col_part = matrix.shape
     panel_width = lower_inv.shape[1]
     panel_count = pivots.shape[0]
@@ -123,8 +130,396 @@
     return current.reshape(row_blocks, row_part, col_blocks, col_part)
 
 
+def to_column(row):
+    n = row.shape[1]
+    eye = lax.broadcasted_iota(jnp.int32, (n, n), 0) == lax.broadcasted_iota(jnp.int32, (n, n), 1)
+    return jnp.max(jnp.where(eye, row, -1.0), axis=1, keepdims=True)
+
+
+def lookup(keys, values, wanted):
+    return jnp.max(jnp.where(keys == wanted, values, -1.0), axis=0, keepdims=True)
+
+
+def plan_kernel(width, order, piv_row_ref, piv_col_ref, slot_ref, pick_ref, source_ref, count_ref):
+    me = lax.axis_index("x") * NZ + lax.axis_index("z")
+    part = width // (NX * NZ)
+    j = lax.broadcasted_iota(jnp.int32, (width, width), 0).astype(jnp.float32)
+    i = lax.broadcasted_iota(jnp.int32, (width, width), 1).astype(jnp.float32)
+    i_row = i[:1]
+    sources, spots, befores = [], [], []
+    for k in range(2):
+        offset = float(k * width)
+        p_row = piv_row_ref[k : k + 1, :].astype(jnp.float32)
+        p_col = piv_col_ref[:, k : k + 1].astype(jnp.float32)
+        chain = jnp.max(jnp.where((p_col == offset + i) & (j < i), j, -1.0), axis=0, keepdims=True)
+        start = jnp.where(chain >= 0.0, chain, i_row)
+
+        def again(state):
+            return state[1] > 0.0
+
+        def jump(state):
+            pointer = state[0]
+            found = lookup(j[:, :1], to_column(pointer), pointer)
+            return found, jnp.max(jnp.abs(found - pointer))
+
+        pointer, _ = lax.while_loop(again, jump, (start, jnp.float32(1.0)))
+        before = offset + pointer
+        before_col = to_column(before)
+        same = p_col == p_row
+        last = jnp.max(jnp.where(same & (j < i), j, -1.0), axis=0, keepdims=True)
+        later = jnp.max(jnp.where(same & (j > i), 1.0, 0.0), axis=0, keepdims=True)
+        anchor = jnp.where(last >= 0.0, lookup(j[:, :1], before_col, last), p_row)
+        spot = jnp.where((later == 0.0) & (p_row >= offset + width), p_row, -5.0)
+        if k == 1:
+            moved = lookup(spots[0], befores[0], anchor)
+            anchor = jnp.where(moved >= 0.0, moved, anchor)
+        sources.append(anchor)
+        spots.append(jnp.max(jnp.where(i == j, spot, -5.0), axis=1, keepdims=True))
+        befores.append(before_col)
+
+    holders, places = [], []
+    for k in range(2):
+        src = sources[k].astype(jnp.int32)
+        within = jnp.bitwise_and(src, width - 1)
+        holders.append((within // part).astype(jnp.float32))
+        places.append(((src // width) * part + jnp.bitwise_and(src, part - 1)).astype(jnp.float32))
+    h_col = [to_column(h) for h in holders]
+    ranks = []
+    for k in range(2):
+        rank = jnp.sum(jnp.where((h_col[k] == holders[k]) & (j < i), 1.0, 0.0), axis=0, keepdims=True)
+        if k == 1:
+            rank = rank + jnp.sum(jnp.where(h_col[0] == holders[1], 1.0, 0.0), axis=0, keepdims=True)
+        ranks.append(rank)
+    most = jnp.maximum(jnp.max(ranks[0]), jnp.max(ranks[1])) + 1.0
+    count_ref[...] = jnp.full(count_ref.shape, most, jnp.float32).astype(jnp.int32)
+    cap = pick_ref.shape[0]
+    k_col = lax.broadcasted_iota(jnp.int32, (cap, width), 0).astype(jnp.float32)
+    pick = jnp.full((cap, 1), -1.0, jnp.float32)
+    for k in range(2):
+        slot_ref[k : k + 1, :] = (holders[k] * float(cap) + jnp.minimum(ranks[k], cap - 1.0)).astype(jnp.int32)
+        mine = jnp.where(holders[k] == me.astype(jnp.float32), ranks[k], -1.0)
+        pick = jnp.maximum(pick, jnp.max(jnp.where(k_col == mine, places[k], -1.0), axis=1, keepdims=True))
+    pick_ref[...] = pick.astype(jnp.int32)
+    rows = source_ref.shape[1]
+    spot_row = lax.broadcasted_iota(jnp.int32, (1, rows), 1)
+    g = ((spot_row // part) * width + me * part + jnp.bitwise_and(spot_row, part - 1)).astype(jnp.float32)
+    first = lookup(spots[1], befores[1], g)
+    g1 = jnp.where(first >= 0.0, first, g)
+    second = lookup(spots[0], befores[0], g1)
+    g0 = jnp.where(second >= 0.0, second, g1)
+    source_ref[...] = jnp.where(g0 == g, -1.0, g0).astype(jnp.int32)
+
+
+def make_plan(pivots, width, order, rows):
+    vmem = pl.BlockSpec(memory_space=pltpu.VMEM)
+    return pl.pallas_call(
+        functools.partial(plan_kernel, width, order),
+        out_shape=(
+            jax.ShapeDtypeStruct((2, width), jnp.int32),
+            jax.ShapeDtypeStruct((CAP, 1), jnp.int32),
+            jax.ShapeDtypeStruct((1, rows), jnp.int32),
+            jax.ShapeDtypeStruct((8, 128), jnp.int32),
+        ),
+        in_specs=[vmem, vmem],
+        out_specs=(vmem, vmem, vmem, vmem),
+        name="row_plan",
+    )(pivots, pivots.T)
+
+
+class Piece:
+    def __init__(self, buf, cols, first, x, z, col, send_sem, recv_sem):
+        self.buf, self.cols, self.first, self.x, self.z, self.col = buf, cols, first, x, z, col
+        self.send_sem, self.recv_sem = send_sem, recv_sem
+        self.rows = buf.shape[1]
+        self.started = []
+        self.na, self.nb = (NX, NZ) if first == "x" else (NZ, NX)
+        self.a, self.b = (x, z) if first == "x" else (z, x)
+
+    def place(self, da, db):
+        return lax.rem(self.a + da + self.na, self.na), lax.rem(self.b + db + self.nb, self.nb)
+
+    def block(self, da, db):
+        a, b = self.place(da, db)
+        return a * NZ + b if self.first == "x" else b * NZ + a
+
+    def device(self, da, db):
+        a, b = self.place(da, db)
+        return (a, b, self.col) if self.first == "x" else (b, a, self.col)
+
+    def copy(self, da, db, to, half, k):
+        block = self.block(da, db)
+        middle = self.rows // 16 * 8
+        low, high = ((0, self.rows), (0, middle), (middle, self.rows))[0 if half is None else half + 1]
+        view = self.buf.at[block, low:high, self.cols[0] : self.cols[1]]
+        return pltpu.make_async_remote_copy(
+            src_ref=view,
+            dst_ref=view,
+            send_sem=self.send_sem.at[block, k],
+            recv_sem=self.recv_sem.at[block, half or 0],
+            device_id=self.device(*to),
+            device_id_type=MESH,
+        )
+
+    def send(self, da, db, to, half, k):
+        copy = self.copy(da, db, to, half, k)
+        copy.start()
+        self.started.append(copy)
+
+    def receive(self, da, db, half):
+        self.copy(da, db, (0, 1), half, 0).wait_recv()
+
+    def along_first(self, d):
+        for s in (1, -1):
+            if d + 1 <= self.na // 2:
+                half = None if d + 1 < self.na // 2 else (1 - s) // 2
+                self.send(-s * d, 0, (s, 0), half, (1 - s) // 2)
+
+    def along_second(self, da, d):
+        for s in (1, -1):
+            if d + 1 <= self.nb // 2:
+                half = None if d + 1 < self.nb // 2 else (1 - s) // 2
+                self.send(da, -s * d, (0, s), half, (1 - s) // 2 + (2 if d == 0 else 0))
+
+    def first_step(self, d):
+        if d == 0:
+            self.along_first(0)
+            self.along_second(0, 0)
+        elif d < self.na // 2:
+            for s in (1, -1):
+                self.receive(-s * d, 0, None)
+            self.along_first(d)
+            for s in (1, -1):
+                self.along_second(-s * d, 0)
+        else:
+            self.receive(d, 0, 0)
+            self.receive(d, 0, 1)
+            self.along_second(d, 0)
+
+    def second_step(self, da, d):
+        if d < self.nb // 2:
+            for s in (1, -1):
+                self.receive(da, -s * d, None)
+            self.along_second(da, d)
+        else:
+            self.receive(da, d, 0)
+            self.receive(da, d, 1)
+
+    def steps(self):
+        work = [(d, functools.partial(self.first_step, d)) for d in range(self.na // 2 + 1)]
+        for d in range(1, self.nb // 2 + 1):
+            for ad in range(self.na // 2 + 1):
+                for da in [0] if ad == 0 else [ad] if ad == self.na // 2 else [-ad, ad]:
+                    work.append((ad + d + 0.5, functools.partial(self.second_step, da, d)))
+        return work
+
+    def finish(self):
+        for copy in self.started:
+            copy.wait_send()
+
+
+def greet(devices):
+    barrier = pltpu.get_barrier_semaphore()
+    for device in devices:
+        pl.semaphore_signal(barrier, inc=1, device_id=device, device_id_type=MESH)
+    pl.semaphore_wait(barrier, len(devices))
+
+
+def run_pieces(pieces, lag):
+    work = []
+    for number, piece in enumerate(pieces):
+        for place, (when, step) in enumerate(piece.steps()):
+            work.append((when + lag[number], number, place, step))
+    work.sort(key=lambda entry: entry[:3])
+    for entry in work:
+        entry[3]()
+    for piece in pieces:
+        piece.finish()
+
+
+def split_three(value):
+    high = value.astype(jnp.bfloat16)
+    rest = value - high.astype(jnp.float32)
+    middle = rest.astype(jnp.bfloat16)
+    low = (rest - middle.astype(jnp.float32)).astype(jnp.bfloat16)
+    return high, middle, low
+
+
+def gather_kernel(matrix_ref, pick_ref, old_ref, new_ref, *sems):
+    x, z, col = lax.axis_index("x"), lax.axis_index("z"), lax.axis_index("pcol")
+    me = x * NZ + z
+    rows, columns = matrix_ref.shape
+    old_ref[pl.ds(me, 1)] = matrix_ref[0 : old_ref.shape[1], :][None]
+    hot = pick_ref[...] == lax.broadcasted_iota(jnp.int32, (CAP, rows), 1)
+    hot = jnp.where(hot, 1.0, 0.0).astype(jnp.bfloat16)
+    for c in range(0, columns, 512):
+        total = jnp.zeros((CAP, 512), jnp.float32)
+        for term in split_three(matrix_ref[:, c : c + 512]):
+            total = total + jnp.dot(hot, term, preferred_element_type=jnp.float32)
+        new_ref[pl.ds(me, 1), :, c : c + 512] = total[None]
+    greet(
+        [
+            (lax.rem(x + 1, NX), z, col),
+            (lax.rem(x + NX - 1, NX), z, col),
+            (x, lax.rem(z + 1, NZ), col),
+            (x, lax.rem(z + NZ - 1, NZ), col),
+        ]
+    )
+    pieces = []
+    for number, buf in enumerate((new_ref, old_ref)):
+        for part, (first, cols) in enumerate((("x", (0, 640)), ("z", (640, 1536)))):
+            s = 4 * number + 2 * part
+            pieces.append(Piece(buf, cols, first, x, z, col, sems[s], sems[s + 1]))
+    run_pieces(pieces, [0.0, 0.0, 0.1, 0.1])
+
+
+def gather_rows(matrix, pick):
+    rows, columns = matrix.shape
+    vmem = pl.BlockSpec(memory_space=pltpu.VMEM)
+    sems = [pltpu.SemaphoreType.DMA((NX * NZ, 4)), pltpu.SemaphoreType.DMA((NX * NZ, 2))]
+    return pl.pallas_call(
+        gather_kernel,
+        out_shape=(
+            jax.ShapeDtypeStruct((NX * NZ, 32, columns), jnp.float32),
+            jax.ShapeDtypeStruct((NX * NZ, CAP, columns), jnp.float32),
+        ),
+        in_specs=[vmem, vmem],
+        out_specs=(vmem, vmem),
+        scratch_shapes=sems * 4,
+        compiler_params=pltpu.CompilerParams(
+            collective_id=0, has_side_effects=True, vmem_limit_bytes=60 * 2**20
+        ),
+        name="gather_rows",
+    )(matrix, pick)
+
+
+def spread_kernel(root, chunks, own_ref, out_ref, send_sem, recv_sem, mate_send, mate_recv):
+    x, z, col = lax.axis_index("x"), lax.axis_index("z"), lax.axis_index("pcol")
+    y, core = col // 2, lax.rem(col, 2)
+    mate = y * 2 + 1 - core
+    up, down = lax.rem(y + 1, 4) * 2 + core, lax.rem(y + 3, 4) * 2 + core
+    away = lax.rem(y - root // 2 + 4, 4)
+    step = own_ref.shape[0] // chunks
+
+    @pl.when(col == root)
+    def _():
+        out_ref[...] = own_ref[...]
+
+    greet([(x, z, mate), (x, z, up), (x, z, down)])
+
+    def copy(c, device, sems, k):
+        view = out_ref.at[c * step : (c + 1) * step]
+        return pltpu.make_async_remote_copy(
+            src_ref=view, dst_ref=view, send_sem=sems[0].at[k], recv_sem=sems[1].at[c],
+            device_id=(x, z, device), device_id_type=MESH,
+        )
+
+    ring, pair = (send_sem, recv_sem), (mate_send, mate_recv)
+
+    @pl.when(core == root % 2)
+    def _():
+        for c in range(chunks):
+            forward = up if c % 2 == 0 else down
+            far = 3 if c % 2 == 0 else 1
+
+            @pl.when(away != 0)
+            def _():
+                copy(c, forward, ring, c).wait_recv()
+
+            @pl.when(away != far)
+            def _():
+                copy(c, forward, ring, c).start()
+
+            copy(c, mate, pair, c).start()
+        for c in range(chunks):
+            forward = up if c % 2 == 0 else down
+            far = 3 if c % 2 == 0 else 1
+
+            @pl.when(away != far)
+            def _():
+                copy(c, forward, ring, c).wait_send()
+
+            copy(c, mate, pair, c).wait_send()
+
+    @pl.when(core != root % 2)
+    def _():
+        for c in range(chunks):
+            copy(c, mate, pair, c).wait_recv()
+
+
+def spread(own, root, chunks, number):
+    vmem = pl.BlockSpec(memory_space=pltpu.VMEM)
+    return pl.pallas_call(
+        functools.partial(spread_kernel, root, chunks),
+        out_shape=jax.ShapeDtypeStruct(own.shape, jnp.float32),
+        in_specs=[vmem],
+        out_specs=vmem,
+        scratch_shapes=[pltpu.SemaphoreType.DMA((chunks,))] * 4,
+        compiler_params=pltpu.CompilerParams(
+            collective_id=number, has_side_effects=True, vmem_limit_bytes=40 * 2**20
+        ),
+        name=f"spread_lower_{root}",
+    )(own)
+
+
+def times(left, right):
+    return jnp.dot(left, right, precision=lax.Precision.HIGH, preferred_element_type=jnp.float32)
+
+
+def balanced(matrix, slots, pick, source, lower_inv, upper_inv):
+    row_blocks, row_part, col_blocks, col_part = matrix.shape
+    width = lower_inv.shape[1]
+    me = lax.axis_index(PROW)
+    col = lax.axis_index("pcol")
+    top = 2 * row_part
+    local = matrix.reshape(row_blocks * row_part, col_blocks * col_part)
+    old, new = gather_rows(local, pick)
+    panels = new.reshape(-1, local.shape[1])[slots.reshape(-1)]
+    source = source[0]
+    old_spot = (source % width) // row_part * top + source // width * row_part + source % row_part
+    moved = old.reshape(-1, local.shape[1])[jnp.maximum(old_spot[top:], 0)]
+    kept = jnp.where((source[top:] >= 0)[:, None], moved, local[top:])
+    top0 = panels[:width]
+    below = jnp.concatenate([panels[width:], kept], axis=0)
+    lower0 = spread(times(below[:, :col_part], upper_inv[0]), 0, 12, 1)
+    solved0 = times(lower_inv[0], top0)
+    chunk0 = jnp.arange(local.shape[1])[None, :] < col_part
+    upper0 = jnp.where(chunk0 & (col == 0), 0.0, solved0)
+    below = below - times(lower0, upper0)
+    lower1 = spread(times(below[width:, :col_part], upper_inv[1]), 1, 11, 2)
+    solved1 = times(lower_inv[1], below[:width])
+    upper1 = jnp.where(chunk0 & (col <= 1), 0.0, solved1)
+    trailing = below[width:] - times(lower1, upper1)
+    first = jnp.where(chunk0 & (col == 0), top0, solved0)
+    second = jnp.where(chunk0 & (col <= 1), below[:width], solved1)
+    head = jnp.where(col == 0, lower0[width:], jnp.where(col == 1, lower1, trailing[:, :col_part]))
+    head1 = jnp.where(col == 0, lower0[:width], second[:, :col_part])
+    own0 = lax.dynamic_slice_in_dim(first, me * row_part, row_part, 0)
+    own1 = jnp.concatenate(
+        [
+            lax.dynamic_slice_in_dim(head1, me * row_part, row_part, 0),
+            lax.dynamic_slice_in_dim(second, me * row_part, row_part, 0)[:, col_part:],
+        ],
+        axis=1,
+    )
+    trailing = jnp.concatenate([head, trailing[:, col_part:]], axis=1)
+    out = jnp.concatenate([own0, own1, trailing], axis=0)
+    return out.reshape(matrix.shape)
+
+
+def local(matrix, pivots, lower_inv, upper_inv):
+    row_blocks, row_part = matrix.shape[:2]
+    width = lower_inv.shape[1]
+    slots, pick, source, most = make_plan(pivots, width, row_blocks * width, row_blocks * row_part)
+    return lax.cond(
+        most[0, 0] <= CAP,
+        lambda m, s, k, r, a, b: balanced(m, s, k, r, a, b),
+        lambda m, s, k, r, a, b: general(m, pivots, a, b),
+        matrix, slots, pick, source, lower_inv, upper_inv,
+    )
+
+
 def solution(mesh):
-    finer = Mesh(mesh.devices.reshape(4, 8, mesh.shape["pcol"]), ("prow_0", "prow_1", "pcol"))
+    finer = Mesh(mesh.devices.reshape(NX, NZ, mesh.shape["pcol"]), ("x", "z", "pcol"))
     in_specs = (P(None, PROW, None, "pcol"), P(), P(), P())
     out_specs = P(None, PROW, None, "pcol")
     return jax.shard_map(local, mesh=finer, in_specs=in_specs, out_specs=out_specs, check_vma=False)

time: 647 us -> 390 us (0.60)
  the two profiles are of different devices: /device:TPU:8 before, /device:TPU:89 now
where the time goes in v1:
time: 390 us; the launch traced here: 387 us
  Pallas kernels  286 us (73%)
  local copies, waits for them, and re-layouts  48.2 us (12%)
  matrix products  25.1 us (6%)
  between operations  14.3 us (4%)
  other arithmetic  7.19 us (2%)
  loops' own time  6.3 us (2%)
    pallas_call x2, Pallas kernels, spread(): pl.pallas_call(functools.partial(spread_kernel, root, chunks), out_shape=...  167 us
    pallas_call x1, Pallas kernels, gather_rows(): pl.pallas_call(gather_kernel, out_shape=(jax.ShapeDtypeStruct((NX * NZ, 3...  114 us
    dot_general x6, matrix products, times(): jnp.dot(left, right, precision=lax.Precision.HIGH, preferred_element_type...  25.1 us
    gather x1, local copies, waits for them, and re-layouts, balanced(): panels = new.reshape(-1, local.shape[1])[slots.reshape(-1)]  12.6 us
    cond x22, local copies, waits for them, and re-layouts  8.25 us

profile of v1, /device:TPU:89, one launch (start us, length us, event | category | flops | bytes accessed | tf_op | source)
XLA Modules:
  0.0 386.6 jit_solution(16661316064550624594)
XLA Ops:
  6.5 1.5 copy.52
  8.1 4.4 %row_plan.1 = (s32[2,512]{1,0:T(2,128)S(1)}, s32[56,1]{1,0:T(8,128)S(1)}, s32[1,384]{1,0:T(1,128)S(1)}, s32[8,128]{1,0:T(8,128)}) custom-call(s32[2,512]{1,0:T(2,128)} %piv_row_ref.1, s32[512,2]{1,0:T(8,128)} %bitcast.202), custom_call_target="tpu_custom_call" | custom-call | tf_op jit(solution)/shard_map/row_plan/pallas_call | solution.py:215
  12.5 1.2 slice.110
  14.3 363.8 %conditional.1 = (f32[24,16,3,512]{3,1,2,0:T(8,128)S(1)}) conditional(s32[]{:T(128)} %bitcast.94, (s32[2,512]{1,0:T(2,128)}, f32[24,16,3,512]{3,1,2,0:T(8,128)}, f32[2,512,512]{2,1,0:T(8,128)}, f32[2,512,512]{2,1,0:T(8,128)}) %tuple.11, (f32[24,16,3,512]{3,1,2,0:T(8,128)}, s32[56,1]{1,0:T(8,128)S(1)}, s32[2,512]{1,0:T(2,128)S(1)}, ...), branch_computations={%region_0.13_spmd, %region_13.14_spmd} | conditional | flops 12491568128 | bytes 310675264 | solution.py:513
  20.2 3.4 copy.54
  23.6 2.5 copy.60
  26.1 114.4 %gather_rows.1 = (f32[32,32,1536]{2,1,0:T(8,128)}, f32[32,56,1536]{2,1,0:T(8,128)}) custom-call(f32[384,1536]{1,0:T(8,128)} %bitcast.191, s32[56,1]{1,0:T(8,128)S(1)} %get-tuple-element.33.pick_ref), custom_call_target="tpu_custom_call" | custom-call | tf_op jit(solution)/shard_map/cond/branch_1_fun/gather_rows/pallas_call | solution.py:379
  140.6 0.1 slice_maximum_fusion
  140.7 7.2 %gather_fusion.1 = f32[352,1536]{1,0:T(8,128)} fusion(f32[1024,1536]{1,0:T(8,128)} %bitcast.183, s32[1024]{0:T(1024)S(1)} %pad_clamp_fusion), kind=kCustom, calls=%fused_computation.31 | custom fusion | bytes 4326784 | tf_op jit(solution)/shard_map/cond/branch_1_fun/gather | solution.py:479
  147.8 0.7 slice.179
  148.6 0.0 copy-start.8
  148.6 1.0 copy.62
  149.6 0.1 compare_reduce_fusion
  149.7 0.5 copy-done.8
  150.2 0.3 broadcast_select_fusion
  150.5 0.0 copy-start.3
  150.5 12.6 %gather_fusion = f32[1024,1536]{1,0:T(8,128)} fusion(f32[1792,1536]{1,0:T(8,128)} %bitcast.180, s32[1024]{0:T(1024)S(1)} %broadcast_clamp_fusion), kind=kCustom, calls=%fused_computation.30 | custom fusion | bytes 12587008 | tf_op jit(solution)/shard_map/cond/branch_1_fun/gather | solution.py:476
  163.1 5.1 %fusion.76 = (f32[512,1536]{1,0:T(8,128)}, f32[512,1536]{1,0:T(8,128)S(1)}) fusion(f32[1024,1536]{1,0:T(8,128)} %gather_fusion), kind=kLoop, calls=%fused_computation.290 | loop fusion | bytes 12582912 | tf_op jit(solution)/shard_map/cond/branch_1_fun/slice | solution.py:481
  168.2 0.0 copy-done.3
  168.3 1.6 copy-done
  169.9 0.0 copy-done.10
  169.9 1.6 fusion.9.own_ref
  171.5 101.6 %spread_lower_0.1 = f32[864,512]{1,0:T(8,128)S(1)} custom-call(f32[864,512]{1,0:T(8,128)S(1)} %fusion.9.own_ref), custom_call_target="tpu_custom_call" | custom-call | tf_op jit(solution)/shard_map/cond/branch_1_fun/spread_lower_0/pallas_call | solution.py:451
  273.1 0.0 copy-start.1
  273.1 0.0 copy-start.4
  273.1 5.1 %convolution_bitcast_fusion.1 = f32[512,1536]{1,0:T(8,128)S(1)} fusion(f32[2,512,512]{2,1,0:T(8,128)} %get-tuple-element.36, f32[1024,1536]{1,0:T(8,128)} %gather_fusion), kind=kOutput, calls=%fused_computation.39 | convolution fusion | flops 2415919104 | bytes 7340032 | tf_op jit(solution)/shard_map/cond/branch_1_fun/dot_general | solution.py:465
  278.2 0.0 copy-start.7
  278.3 1.7 copy-done.7
  280.0 0.0 copy-done.1
  280.0 0.0 copy-done.4
  280.0 6.6 %fusion = f32[864,1536]{1,0:T(8,128)} fusion(f32[352,1536]{1,0:T(8,128)S(1)} %copy-done.4, f32[512,1536]{1,0:T(8,128)S(1)} %copy-done.1, f32[864,512]{1,0:T(8,128)S(1)} %spread_lower_0.1, f32[512,1536]{1,0:T(8,128)S(1)} %convolution_bitcast_fusion.1, pred[1536]{0:T(1024)(128)(4,1)S(1)} %fusion.27), kind=kOutput, calls=%fused_computation.37 | convolution fusion | flops 4080304128 | bytes 15533568 | tf_op jit(solution)/shard_map/cond/branch_1_fun/dot_general | solution.py:465
  286.6 7.7 %slice_select_fusion = (f32[512,1536]{1,0:T(8,128)}, f32[512,1536]{1,0:T(8,128)S(1)}) fusion(f32[864,1536]{1,0:T(8,128)} %fusion, pred[1536]{0:T(1024)(128)(4,1)S(1)} %fusion.26, f32[2,512,512]{2,1,0:T(8,128)} %get-tuple-element.36), kind=kOutput, calls=%fused_computation.44 | convolution fusion | flops 2416705536 | bytes 13633024 | tf_op jit(solution)/shard_map/cond/branch_1_fun/dot_general | solution.py:465
  294.3 0.0 copy-done.2
  294.3 0.0 copy-done.11
  294.3 0.8 fusion.15.own_ref
  295.1 65.1 %spread_lower_1.1 = f32[352,512]{1,0:T(8,128)S(1)} custom-call(f32[352,512]{1,0:T(8,128)S(1)} %fusion.15.own_ref), custom_call_target="tpu_custom_call" | custom-call | tf_op jit(solution)/shard_map/cond/branch_1_fun/spread_lower_1/pallas_call | solution.py:451
  360.2 3.3 fusion.4
  363.5 2.2 fusion.24
  365.7 2.4 slice.183
  368.1 0.1 slice.98
  368.2 0.8 dynamic-slice_select_fusion.1
  369.0 0.8 dynamic-slice
  369.8 1.0 dynamic-slice_select_fusion
  370.8 2.7 maximum_maximum_fusion
  373.5 3.5 reshape.946
  377.0 0.9 copy.57
  378.1 0.0 copy-start.13
  378.1 1.4 copy-done.13
  (14 shorter events, 0.1 us)
Async XLA Ops:
  148.6 1.6 copy-start.8
  150.5 17.8 %copy-start.3 = (f32[352,1536]{1,0:T(8,128)}, f32[352,1536]{1,0:T(8,128)S(1)}, u32[]{:S(2)}) copy-start(f32[352,1536]{1,0:T(8,128)S(1)} %broadcast_select_fusion) | copy-start | bytes 6488068 | tf_op jit(solution)/shard_map/cond
  163.1 6.7 %copy-start.10 = (f32[2,512,512]{2,1,0:T(8,128)S(1)}, f32[2,512,512]{2,1,0:T(8,128)}, u32[]{:S(2)}) copy-start(f32[2,512,512]{2,1,0:T(8,128)} %get-tuple-element.39) | copy-start | bytes 6291460 | tf_op jit(solution)/shard_map/cond
  168.2 1.6 copy-start
  273.1 6.9 %copy-start.1 = (f32[512,1536]{1,0:T(8,128)S(1)}, f32[512,1536]{1,0:T(8,128)}, u32[]{:S(2)}) copy-start(f32[512,1536]{1,0:T(8,128)} %copy-done) | copy-start | bytes 9437188 | tf_op jit(solution)/shard_map/cond
  273.1 6.9 %copy-start.4 = (f32[352,1536]{1,0:T(8,128)S(1)}, f32[352,1536]{1,0:T(8,128)}, u32[]{:S(2)}) copy-start(f32[352,1536]{1,0:T(8,128)} %copy-done.3) | copy-start | bytes 6488068 | tf_op jit(solution)/shard_map/cond
  278.2 1.7 copy-start.7
  286.6 7.8 %copy-start.2 = (f32[864,1536]{1,0:T(8,128)S(1)}, f32[864,1536]{1,0:T(8,128)}, u32[]{:S(2)}) copy-start(f32[864,1536]{1,0:T(8,128)} %fusion) | copy-start | bytes 15925252 | tf_op jit(solution)/shard_map/cond
  286.6 7.8 %copy-start.11 = (f32[2,512,512]{2,1,0:T(8,128)S(1)}, f32[2,512,512]{2,1,0:T(8,128)}, u32[]{:S(2)}) copy-start(f32[2,512,512]{2,1,0:T(8,128)} %get-tuple-element.39) | copy-start | bytes 6291460 | tf_op jit(solution)/shard_map/cond
  365.7 5.0 %slice-start = ((f32[352,1536]{1,0:T(8,128)}), f32[352,1024]{1,0:T(8,128)S(1)}, s32[]{:S(2)}) async-start(f32[352,1536]{1,0:T(8,128)} %fusion.4), calls=%async_computation.14 | async-start | bytes 2883584 | tf_op jit(solution)/shard_map/cond/branch_1_fun/slice | solution.py:504
  378.1 1.4 copy-start.13
